TPU v7x, 32 devices: a whole 2x2x4 slice. The times are simulated.
32 devices in a mesh: blk: 8 (over z, y), kv: 4 (over x, core).
Axes of the slice: x: 2, y: 2, z: 4, core: 2. Of those that a mesh axis runs over, the one named last changes fastest.
Arguments:
- queries: bfloat16 [2048, 16, 2, 128], P('blk', 'kv'), may hold values from -80 to 80
- suffix_kv: bfloat16 [2048, 2, 16, 128], P('blk', None, 'kv'), may hold values from -4 to 4
- cache: bfloat16 [16, 2, 32, 16, 128], P('blk', None, None, 'kv'), may hold values from -4 to 4
- page_table: int32 [16], replicated, may hold values from 0 to 15, each once
- req_prefix: int32 [32], P('blk'), may hold values from 0 to 3
- suffix_len: int32 [8, 4], P('blk'), may hold values from 1 to 128, 256 in all within a row
- att_experts: int32 [2048, 2], P('blk'), may hold values from 0 to 7, all different within a row
- att_gates: float32 [2048, 2], P('blk'), may hold values from 0.2 to 1
- out_proj: bfloat16 [8, 2048, 2048], P(None, 'blk', 'kv'), may hold values from -0.375 to 0.375
Outputs:
- attn_out: bfloat16 [2048, 2048], P('blk', 'kv')
Inputs may be any that keep to these rules, and one draw needn't show every extreme that they name: `page_table`: every physical page holds exactly one page of one prefix. `suffix_len`: each row adds up to 256, so requests never span two indices of blk; the longest suffix of each row is exactly 128. `att_experts`: the experts of one token differ.
All inputs are finite; a program needn't handle non-finite values.
Results may differ from a plain program's by a relative error of at most 0.015.
Values may be sent and summed in bfloat16 or wider, within the bound.
A program may use at most 128 MiB of HBM per device.

v0:
```python
import math

import jax
import jax.numpy as jnp
from jax import lax
from jax.sharding import PartitionSpec as P

PREFIXES = 4


MASKED_SCORE = -1e30


def absorb(carried, query_rows, key_rows, value_rows, allowed):
    running_max, denominator, numerator = carried
    scaling = 1.0 / math.sqrt(query_rows.shape[-1])
    scores = (
        jnp.einsum("thjd,khd->thjk", query_rows, key_rows, preferred_element_type=jnp.float32)
        * scaling
    )
    visible = allowed[:, None, None, :]
    scores = jnp.where(visible, scores, MASKED_SCORE)
    new_max = jnp.maximum(running_max, jnp.max(scores, axis=3))
    weights = jnp.where(visible, jnp.exp(scores - new_max[..., None]), 0.0)
    factor = jnp.exp(running_max - new_max)
    denominator = denominator * factor + jnp.sum(weights, axis=3)
    numerator = numerator * factor[..., None] + jnp.einsum(
        "thjk,khd->thjd",
        weights.astype(jnp.bfloat16),
        value_rows,
        preferred_element_type=jnp.float32,
    )
    return (new_max, denominator, numerator)


def body(
    queries, suffix_kv, cache, page_table, req_prefix, suffix_len, att_experts, att_gates, out_proj
):
    tok_count = queries.shape[0]
    head_count = queries.shape[1]
    slot_count = queries.shape[2]
    head_width = queries.shape[3]
    page_rows = cache.shape[2]
    total_pages = page_table.shape[0]
    per_prefix = total_pages // PREFIXES
    page_ids = jnp.arange(total_pages, dtype=jnp.int32)
    owner_match = page_table[None, :] == page_ids[:, None]
    page_prefix = jnp.sum(jnp.where(owner_match, (page_ids // per_prefix)[None, :], 0), axis=1)
    lengths = suffix_len[0]
    request_ends = jnp.cumsum(lengths)
    positions = jnp.arange(tok_count, dtype=jnp.int32)
    request_of = jnp.sum((positions[:, None] >= request_ends[None, :]).astype(jnp.int32), axis=1)
    request_ids = jnp.arange(lengths.shape[0], dtype=jnp.int32)
    token_prefix = jnp.sum(
        jnp.where(request_of[:, None] == request_ids[None, :], req_prefix[None, :], 0), axis=1
    )
    own_keys = suffix_kv[:, 0]
    own_values = suffix_kv[:, 1]
    block_rows = min(tok_count, 512)
    blocks = tok_count // block_rows

    def suffix_block(block_index):
        allowed = (request_of[:, None] == request_of[None, :]) & (
            positions[:, None] >= positions[None, :]
        )
        initial = (
            jnp.full((block_rows, head_count, slot_count), MASKED_SCORE, jnp.float32),
            jnp.zeros((block_rows, head_count, slot_count), jnp.float32),
            jnp.zeros((block_rows, head_count, slot_count, head_width), jnp.float32),
        )
        return absorb(initial, queries, own_keys, own_values, allowed)

    first_max, first_sum, first_acc = lax.map(suffix_block, jnp.arange(blocks, dtype=jnp.int32))
    carried = (
        first_max.reshape(tok_count, head_count, slot_count),
        first_sum.reshape(tok_count, head_count, slot_count),
        first_acc.reshape(tok_count, head_count, slot_count, head_width),
    )
    key_cap = max(1, 256 // page_rows)
    page_piece = lax.all_gather(cache, "blk", axis=0, tiled=True)
    number = page_piece.shape[0]
    pages_tile = 1
    for candidate in range(1, min(number, key_cap) + 1):
        if number % candidate == 0:
            pages_tile = candidate
    tile_owners = page_prefix.reshape(number // pages_tile, pages_tile)
    page_tiles = page_piece.reshape(
        number // pages_tile, pages_tile, 2, page_rows, head_count, head_width
    )

    def absorb_tile(current, tile_item):
        one_tile, tile_owner = tile_item
        tile_keys = one_tile[:, 0].reshape(pages_tile * page_rows, head_count, head_width)
        tile_values = one_tile[:, 1].reshape(pages_tile * page_rows, head_count, head_width)
        key_prefix = jnp.repeat(tile_owner, page_rows)
        allowed = token_prefix[:, None] == key_prefix[None, :]
        updated = absorb(current, queries, tile_keys, tile_values, allowed)
        return (updated, None)

    finished, ignored = lax.scan(absorb_tile, carried, (page_tiles, tile_owners))
    running_max, denominator, numerator = finished
    attention = (numerator / denominator[..., None]).astype(jnp.bfloat16)
    expert_count = out_proj.shape[0]
    expert_ids = jnp.arange(expert_count, dtype=jnp.int32)
    gate_table = jnp.where(
        att_experts[:, :, None] == expert_ids[None, None, :], att_gates[:, :, None], 0.0
    )
    combined = jnp.zeros((expert_count, tok_count, head_count, head_width), jnp.float32)
    for slot_index in range(slot_count):
        combined = (
            combined
            + gate_table[:, slot_index, :].T[:, :, None, None]
            * attention[:, :, slot_index, :].astype(jnp.float32)[None]
        )
    combined = combined.reshape(expert_count, tok_count, head_count * head_width).astype(
        jnp.bfloat16
    )
    column_sums = jnp.einsum(
        "etf,ecf->tc",
        combined,
        lax.all_gather(out_proj, "blk", axis=1, tiled=True),
        preferred_element_type=jnp.float32,
    )
    return lax.psum_scatter(column_sums.astype(jnp.bfloat16), "kv", scatter_dimension=1, tiled=True)


def solution(mesh):
    in_specs = (
        P("blk", "kv", None, None),
        P("blk", None, "kv", None),
        P("blk", None, None, "kv", None),
        P(),
        P("blk"),
        P("blk", None),
        P("blk", None),
        P("blk", None),
        P(None, "blk", "kv"),
    )
    out_specs = P("blk", "kv")
    return jax.shard_map(body, mesh=mesh, in_specs=in_specs, out_specs=out_specs, check_vma=False)
```

profile of v0, /device:TPU:0, one launch (start us, length us, event | category | flops | bytes accessed | tf_op | source)
XLA Modules:
  0.0 322.0 jit_solution(16806996996497541259)
XLA Ops:
  6.5 1.7 copy.50
  8.3 0.7 all-gather.5.cloned.1.call-update
  9.1 0.2 reduce-window.8
  9.5 0.2 fusion.39
  9.7 0.5 fusion.19
  10.3 0.5 fusion.21
  10.8 1.0 fusion.22
  11.8 0.3 copy.51
  12.2 0.3 copy-done.6
  12.8 39.6 %all-gather.3.cloned.1.call-done = bf16[16,2,32,4,128]{4,2,3,1,0:T(8,128)(2,1)} async-done(((bf16[2,2,32,4,128]{4,2,3,1,0:T(8,128)(2,1)}), bf16[16,2,32,4,128]{4,2,3,1,0:T(8,128)(2,1)}) %all-gather.3.cloned.1.call-update) | async-done | bytes 1048592 | tf_op jit(solution)/shard_map/all_gather | solution.py:80
  52.4 6.7 %while.2 = (s32[]{:T(128)}, f32[256,4,2]{0,2,1:T(2,128)S(1)}, f32[256,4,2]{0,2,1:T(2,128)S(1)}, f32[256,4,2,128]{0,3,2,1:T(8,128)S(1)}, s32[256]{0:T(256)S(1)}, ...) while((s32[]{:T(128)}, f32[256,4,2]{0,2,1:T(2,128)S(1)}, ...), condition=%wide.region_9.10_spmd, body=%wide.region_6.9_spmd.sunk | while | flops 275845120 | bytes 11933377 | solution.py:100
  52.6 1.1 copy_bitcast_fusion.6
  53.8 0.5 fusion.59
  54.3 0.5 fusion.60
  54.8 0.9 fusion.61
  56.0 1.1 copy_bitcast_fusion.6
  57.1 0.5 fusion.59
  57.6 0.5 fusion.60
  58.2 0.9 fusion.61
  59.3 0.2 copy.54
  59.5 0.2 copy.55
  59.7 221.2 %all-gather.5.cloned.1.call-done = bf16[8,2048,512]{2,1,0:T(8,128)(2,1)} async-done(((bf16[8,256,512]{2,1,0:T(8,128)(2,1)}), bf16[8,2048,512]{2,1,0:T(8,128)(2,1)}) %all-gather.5.cloned.1.call-update) | async-done | bytes 16777232 | tf_op jit(solution)/shard_map/all_gather | solution.py:121
  280.9 11.3 %fusion.14 = bf16[256,2048]{1,0:T(8,128)(2,1)} fusion(bf16[8,2048,512]{2,1,0:T(8,128)(2,1)} %all-gather.5.cloned.1.call-done, f32[256,512]{1,0:T(8,128)S(1)} %copy.55, f32[8,256]{1,0:T(8,128)S(1)} %get-tuple-element.136, f32[256,512]{1,0:T(8,128)S(1)} %copy.54, f32[8,256]{1,0:T(8,128)S(1)} %get-tuple-element.135), kind=kOutput, calls=%fused_computation.24 | convolution fusion | flops 4299685888 | bytes 18890752 | tf_op jit(solution)/shard_map/etf,ecf->tc/dot_general | solution.py:118
  292.3 23.2 %reduce-scatter.2.cloned.1.call-done = bf16[256,512]{1,0:T(8,128)(2,1)} async-done(((bf16[256,2048]{1,0:T(8,128)(2,1)}), bf16[256,512]{1,0:T(8,128)(2,1)}) %reduce-scatter.2.cloned.1.call-update) | async-done | bytes 262160 | tf_op jit(solution)/shard_map/reduce_scatter | solution.py:124
  (48 shorter events, 1.6 us)
Async XLA Ops:
  6.5 2.5 copy-start.1
  6.5 2.6 copy-start.5
  6.5 3.0 copy-start
  6.5 45.8 %all-gather.3.cloned.1.call-start = ((), (), s32[]{:S(2)}) async-start(), calls=%async_computation.1 | async-start | bytes 1179648 | tf_op jit(solution)/shard_map/all_gather | solution.py:80
  8.2 272.7 %all-gather.5.cloned.1.call-start = ((), (), s32[]{:S(2)}) async-start(), calls=%async_computation.2 | async-start | bytes 18874368 | tf_op jit(solution)/shard_map/all_gather | solution.py:121
  9.0 306.5 %reduce-scatter.2.cloned.1.call-start = ((), (), s32[]{:S(2)}) async-start(), calls=%async_computation.3 | async-start | bytes 1310720 | tf_op jit(solution)/shard_map/reduce_scatter | solution.py:124
  11.8 0.7 copy-start.6
  11.8 0.8 copy-start.4
  11.8 0.9 copy-start.2
  11.8 0.9 copy-start.3
Sparse Core Ops, SparseCore 0:
  9.5 42.8 all-gather.2
  54.5 226.3 all-gather.4
  292.4 23.0 reduce-scatter.1
where the time goes:
time: 322 us
  waiting for transfers between devices  285 us (89%)
  matrix products  15.5 us (5%)
  between operations  13.3 us (4%)
  local copies, waits for them, and re-layouts  5.62 us (2%)
    all_gather x1, waiting for transfers between devices, body(): lax.all_gather(out_proj, 'blk', axis=1, tiled=True)  221 us
    all_gather x1, waiting for transfers between devices, body(): page_piece = lax.all_gather(cache, 'blk', axis=0, tiled=True)  39.6 us
    reduce_scatter x1, waiting for transfers between devices, body(): lax.psum_scatter(column_sums.astype(jnp.bfloat16), 'kv', scatter_dimensio...  23.2 us
    dot_general x1, matrix products, body(): jnp.einsum('etf,ecf->tc', combined, lax.all_gather(out_proj, 'blk', axis=...  11.3 us
  transfers between devices with their start and end apart: 3, of which 3 were waited for; matrix products, arithmetic and copies ran while one was open for 3% of the time, Pallas kernels for 0%

commit v1 on v0

--- a/solution.py
+++ b/solution.py
@@ -1,8 +1,11 @@
+import functools
 import math
 
 import jax
 import jax.numpy as jnp
 from jax import lax
+from jax.experimental import pallas as pl
+from jax.experimental.pallas import tpu as pltpu
 from jax.sharding import PartitionSpec as P
 
 PREFIXES = 4
@@ -124,6 +127,299 @@
     return lax.psum_scatter(column_sums.astype(jnp.bfloat16), "kv", scatter_dimension=1, tiled=True)
 
 
+MESH = pl.DeviceIdType.MESH
+F32 = jnp.float32
+BF16 = jnp.bfloat16
+NT = (((1,), (1,)), ((), ()))
+
+
+def fused_kernel(
+    pt_ref, rp_ref, sl_ref, ex_ref, ga_ref, q_ref, s_ref, c_ref, w_ref, o_ref,
+    cbuf, wbuf, ubuf, tbl, bias, comb, pbuf, prec, fin,
+    loc_sem, cz_send, cz_recv, cy_send, cy_recv, w_send, w_recv,
+    t_send, t_recv, u_send, u_recv, p_send, p_recv, o_send, o_recv,
+):
+    blk = lax.axis_index("blk")
+    k = lax.axis_index("kv")
+    z = blk // 2
+    y = blk % 2
+    heads = 4
+    tok = q_ref.shape[0]
+    cached = cbuf.shape[0] * cbuf.shape[1] * cbuf.shape[3]
+    page_rows = cbuf.shape[3]
+    pages = pt_ref.shape[0]
+    reqs = rp_ref.shape[0]
+    partner = z * 2 + (1 - y)
+
+    def zpeer(d):
+        return lax.rem(z + d, 4)
+
+    barrier = pltpu.get_barrier_semaphore()
+    for dz in range(4):
+        for dk in range(4):
+            if dz or dk:
+                pl.semaphore_signal(
+                    barrier, inc=1, device_id=(zpeer(dz) * 2 + y, lax.rem(k + dk, 4)), device_id_type=MESH
+                )
+    pl.semaphore_signal(barrier, inc=1, device_id=(partner, k), device_id_type=MESH)
+    pl.semaphore_wait(barrier, 16)
+
+    def remote(src, dst, send, recv, to):
+        return pltpu.make_async_remote_copy(
+            src_ref=src, dst_ref=dst, send_sem=send, recv_sem=recv, device_id=to, device_id_type=MESH
+        )
+
+    def cz(d, slot):
+        return remote(c_ref, cbuf.at[slot], cz_send.at[d - 1], cz_recv.at[d - 1], (zpeer(d) * 2 + y, k))
+
+    def cy(d):
+        slot = lax.rem(z - d + 4, 4) * 2 + y
+        source = c_ref if d == 0 else cbuf.at[slot]
+        return remote(source, cbuf.at[slot], cy_send.at[d], cy_recv.at[d], (partner, k))
+
+    for d in (1, 3, 2):
+        cz(d, blk).start()
+    cy(0).start()
+    own_c = pltpu.make_async_copy(c_ref, cbuf.at[blk], loc_sem.at[0])
+    own_c.start()
+    own_w = pltpu.make_async_copy(w_ref, wbuf.at[0], loc_sem.at[1])
+    own_w.start()
+
+    lane = lax.broadcasted_iota(jnp.int32, (tok, 128), 1)
+    hot0 = jnp.where(lane == ex_ref[:, 0:1], 1.0, 0.0)
+    hot1 = jnp.where(lane - 8 == ex_ref[:, 1:2], 1.0, 0.0)
+    hot = jnp.where(lane < 8, hot0, jnp.where(lane < 16, hot1, 0.0))
+    tbl[z] = hot.T[0:16].astype(BF16)
+
+    def tcopy(d, slot):
+        return remote(tbl.at[slot], tbl.at[slot], t_send.at[d - 1], t_recv.at[d - 1], (zpeer(d) * 2 + y, k))
+
+    row = lax.broadcasted_iota(jnp.int32, (tok, 128), 0)
+    colq = lax.broadcasted_iota(jnp.int32, (8, tok), 1)
+    req_row = jnp.zeros((tok, 128), jnp.int32)
+    req_col = jnp.zeros((8, tok), jnp.int32)
+    pref_row = jnp.full((tok, 128), rp_ref[0], jnp.int32)
+    end = jnp.int32(0)
+    for r in range(reqs):
+        end = end + sl_ref[0, r]
+        past = row >= end
+        req_row = req_row + jnp.where(past, 1, 0)
+        req_col = req_col + jnp.where(colq >= end, 1, 0)
+        if r + 1 < reqs:
+            pref_row = jnp.where(past, rp_ref[r + 1], pref_row)
+    page_of = lax.broadcasted_iota(jnp.int32, (8, cached), 1) // page_rows
+    key_prefix = jnp.zeros((8, cached), jnp.int32)
+    for entry in range(pages):
+        key_prefix = jnp.where(page_of == pt_ref[entry], entry // (pages // PREFIXES), key_prefix)
+    bias[:, 0:cached] = jnp.where(pref_row[:, 0:1] == key_prefix[0:1, :], 0.0, MASKED_SCORE)
+    keep = jnp.logical_and(req_row[:, 0:1] == req_col[0:1, :], row[:, 0:1] >= colq[0:1, :])
+    bias[:, cached:] = jnp.where(keep, 0.0, MASKED_SCORE)
+
+    for d in (1, 3, 2):
+        cz(d, lax.rem(z - d + 4, 4) * 2 + y).wait_recv()
+        cy(d).start()
+    own_c.wait()
+
+    def wcopy():
+        return remote(w_ref, wbuf.at[1], w_send.at[0], w_recv.at[0], (partner, k))
+
+    wcopy().start()
+    for d in (1, 2, 3):
+        tcopy(d, z).start()
+
+    def ycopy_in(d):
+        slot = lax.rem(z - d + 4, 4) * 2 + (1 - y)
+        return remote(cbuf.at[slot], cbuf.at[slot], cy_send.at[d], cy_recv.at[d], (partner, k))
+
+    for d in range(4):
+        ycopy_in(d).wait_recv()
+
+    def ucopy(h, d, slot):
+        return remote(
+            ubuf.at[slot, h], ubuf.at[slot, h], u_send.at[h, d - 1], u_recv.at[h, d - 1], (zpeer(d) * 2 + y, k)
+        )
+
+    factor = math.log2(math.e) / math.sqrt(128)
+    for h in range(heads):
+        span = slice(h * 128, (h + 1) * 128)
+        keys = cbuf[:, :, 0, :, span].reshape(cached, 128)
+        values = cbuf[:, :, 1, :, span].reshape(cached, 128)
+        skeys = s_ref[:, span]
+        svalues = s_ref[:, heads * 128 + h * 128 : heads * 128 + (h + 1) * 128]
+        for j in range(2):
+            place = slice((h * 2 + j) * 128, (h * 2 + j + 1) * 128)
+            query = q_ref[:, place]
+            sa = lax.dot_general(query, keys, NT, preferred_element_type=F32) * factor + bias[:, 0:cached]
+            sb = lax.dot_general(query, skeys, NT, preferred_element_type=F32) * factor + bias[:, cached:]
+            top = jnp.maximum(jnp.max(sa, axis=1, keepdims=True), jnp.max(sb, axis=1, keepdims=True))
+            pa = jnp.exp2(sa - top)
+            pb = jnp.exp2(sb - top)
+            den = jnp.sum(pa, axis=1, keepdims=True) + jnp.sum(pb, axis=1, keepdims=True)
+            num = jnp.dot(pa.astype(BF16), values, preferred_element_type=F32) + jnp.dot(
+                pb.astype(BF16), svalues, preferred_element_type=F32
+            )
+            att = (num / den).astype(BF16).astype(F32)
+            ubuf[z, h, :, j * 128 : (j + 1) * 128] = (att * ga_ref[:, j : j + 1]).astype(BF16)
+        for d in (1, 3, 2):
+            ucopy(h, d, z).start()
+    own_w.wait()
+
+    sel_row = lax.broadcasted_iota(jnp.int32, (16, 16 * 128), 0)
+    sel_col = lax.broadcasted_iota(jnp.int32, (16, 16 * 128), 1) // 128
+    select = jnp.where(sel_row == sel_col, 1.0, 0.0).astype(BF16)
+
+    def pcopy(i, e):
+        q = lax.rem(k + e, 4)
+        rows = pl.ds(pl.multiple_of(q * 64, 64), 64)
+        return remote(
+            pbuf.at[i, rows], prec.at[i, e - 1], p_send.at[i, e - 1], p_recv.at[i, e - 1], (blk, q)
+        )
+
+    def half_of(i):
+        half = jnp.where(i < 4, y, 1 - y)
+        return pl.ds(pl.multiple_of(half * 256, 256), 256)
+
+    def ocopy(i):
+        d = lax.rem(i, 4)
+        rows = pl.ds(pl.multiple_of(k * 64, 64), 64)
+        to = lax.rem(z - d + 4, 4) * 2 + y
+        return remote(fin.at[i], o_ref.at[rows, half_of(i)], o_send.at[i], o_recv.at[i // 4, k], (to, z))
+
+    def step(i, carry):
+        @pl.when(i < 8)
+        def _():
+            d = lax.rem(i, 4)
+            source = lax.rem(z - d + 4, 4)
+
+            @pl.when(i < 4)
+            def _():
+                @pl.when(d > 0)
+                def _():
+                    for h in range(heads):
+                        remote(
+                            ubuf.at[source, h], ubuf.at[source, h], u_send.at[h, d - 1], u_recv.at[h, d - 1], (blk, k)
+                        ).wait_recv()
+                    remote(tbl.at[source], tbl.at[source], t_send.at[d - 1], t_recv.at[d - 1], (blk, k)).wait_recv()
+
+                mask = lax.dot_general(
+                    tbl[source], select, (((0,), (0,)), ((), ())), preferred_element_type=F32
+                ).astype(BF16)
+                for h in range(heads):
+                    u0 = ubuf[source, h, :, 0:128]
+                    u1 = ubuf[source, h, :, 128:256]
+                    for e in range(8):
+                        comb[d, :, e * 512 + h * 128 : e * 512 + (h + 1) * 128] = (
+                            u0 * mask[:, e * 128 : (e + 1) * 128] + u1 * mask[:, (8 + e) * 128 : (9 + e) * 128]
+                        )
+
+            @pl.when(i == 4)
+            def _():
+                wcopy().wait_recv()
+
+            part = jnp.zeros((tok, 256), F32)
+            for e in range(8):
+                part = part + lax.dot_general(
+                    comb[d, :, e * 512 : (e + 1) * 512], wbuf[i // 4, e], NT, preferred_element_type=F32
+                )
+            pbuf[i] = part.astype(BF16)
+            for e in (2, 3, 1):
+                pcopy(i, e).start()
+
+        @pl.when(i > 0)
+        def _():
+            p = i - 1
+            own = pl.ds(pl.multiple_of(k * 64, 64), 64)
+            total = pbuf[p, own].astype(F32)
+            for e in (1, 2, 3):
+                pcopy(p, e).wait_recv()
+                total = total + prec[p, e - 1].astype(F32)
+            here = jnp.logical_and(lax.rem(p, 4) == 0, k == z)
+
+            @pl.when(here)
+            def _():
+                o_ref[own, half_of(p)] = total.astype(BF16)
+
+            @pl.when(jnp.logical_not(here))
+            def _():
+                fin[p] = total.astype(BF16)
+                ocopy(p).start()
+
+        return carry
+
+    lax.fori_loop(0, 9, step, 0)
+
+    for g in range(2):
+        for q in range(4):
+            rows = pl.ds(q * 64, 64)
+
+            @pl.when(jnp.logical_or(k != z, k != q))
+            def _():
+                remote(
+                    fin.at[0], o_ref.at[rows, half_of(g * 4)], o_send.at[0], o_recv.at[g, q], (blk, k)
+                ).wait_recv()
+
+    def drain(i, carry):
+        for e in (1, 2, 3):
+            pcopy(i, e).wait_send()
+
+        @pl.when(jnp.logical_or(lax.rem(i, 4) != 0, k != z))
+        def _():
+            ocopy(i).wait_send()
+
+        return carry
+
+    lax.fori_loop(0, 8, drain, 0)
+    for d in (1, 2, 3):
+        cz(d, blk).wait_send()
+        tcopy(d, z).wait_send()
+        for h in range(heads):
+            ucopy(h, d, z).wait_send()
+    for d in range(4):
+        cy(d).wait_send()
+    wcopy().wait_send()
+
+
+def fused_body(
+    queries, suffix_kv, cache, page_table, req_prefix, suffix_len, att_experts, att_gates, out_proj
+):
+    tok, heads, slots, width = queries.shape
+    local_pages, _, page_rows = cache.shape[:3]
+    experts, columns, features = out_proj.shape
+    vmem = pl.BlockSpec(memory_space=pltpu.VMEM)
+    smem = pl.BlockSpec(memory_space=pltpu.SMEM)
+    dma = pltpu.SemaphoreType.DMA
+    return pl.pallas_call(
+        fused_kernel,
+        out_shape=jax.ShapeDtypeStruct((tok, 2 * columns), BF16),
+        in_specs=[smem, smem, smem, vmem, vmem, vmem, vmem, vmem, pl.BlockSpec(memory_space=pl.ANY)],
+        out_specs=vmem,
+        scratch_shapes=[
+            pltpu.VMEM((8, local_pages, 2, page_rows, heads * width), BF16),
+            pltpu.VMEM((2, experts, columns, features), BF16),
+            pltpu.VMEM((4, heads, tok, slots * width), BF16),
+            pltpu.VMEM((4, slots * experts, tok), BF16),
+            pltpu.VMEM((tok, 8 * local_pages * page_rows + tok), F32),
+            pltpu.VMEM((4, tok, experts * features), BF16),
+            pltpu.VMEM((8, tok, columns), BF16),
+            pltpu.VMEM((8, 3, tok // 4, columns), BF16),
+            pltpu.VMEM((8, tok // 4, columns), BF16),
+            dma((2,)), dma((3,)), dma((3,)), dma((4,)), dma((4,)), dma((1,)), dma((1,)),
+            dma((3,)), dma((3,)), dma((heads, 3)), dma((heads, 3)),
+            dma((8, 3)), dma((8, 3)), dma((8,)), dma((2, 4)),
+        ],
+        compiler_params=pltpu.CompilerParams(
+            collective_id=0, has_side_effects=True, vmem_limit_bytes=48 * 1024 * 1024
+        ),
+        cost_estimate=pl.CostEstimate(flops=6 * 10**9, bytes_accessed=8 * 10**6, transcendentals=2 * 10**6),
+    )(
+        page_table, req_prefix, suffix_len, att_experts, att_gates,
+        queries.reshape(tok, heads * slots * width),
+        suffix_kv.reshape(tok, 2 * heads * width),
+        cache.reshape(local_pages, 2, page_rows, heads * width),
+        out_proj,
+    )
+
+
 def solution(mesh):
     in_specs = (
         P("blk", "kv", None, None),
@@ -137,4 +433,7 @@
         P(None, "blk", "kv"),
     )
     out_specs = P("blk", "kv")
-    return jax.shard_map(body, mesh=mesh, in_specs=in_specs, out_specs=out_specs, check_vma=False)
+    chosen = body
+    if mesh.shape["blk"] == 2 * mesh.shape["kv"] and mesh.shape["kv"] == 4:
+        chosen = fused_body
+    return jax.shard_map(chosen, mesh=mesh, in_specs=in_specs, out_specs=out_specs, check_vma=False)

time: 322 us -> 95.2 us (0.30)
  waiting for transfers between devices: 285 us -> 0 us
  Pallas kernels: 0 us -> 87.1 us
  matrix products: 15.5 us -> 0 us
  between operations: 13.3 us -> 0.07 us
    all_gather x2 -> x0, waiting for transfers between devices: 261 us -> none  [the longest x1 221 us: body(): lax.all_gather(out_proj, 'blk', axis=1, tiled=True)]
    pallas_call x0 -> x1, Pallas kernels: none -> 87.1 us  [fused_body(): pl.pallas_call(fused_kernel, out_shape=jax.ShapeDtypeStruct((tok, 2 * col...]
    reduce_scatter x1 -> x0, waiting for transfers between devices: 23.2 us -> none  [body(): lax.psum_scatter(column_sums.astype(jnp.bfloat16), 'kv', scatter_dimensio...]
    dot_general x7 -> x0, matrix products: 15.5 us -> none  [the longest x1 11.3 us: body(): jnp.einsum('etf,ecf->tc', combined, lax.all_gather(out_proj, 'blk', axis=...]
    reshape x1 -> x3, local copies, waits for them, and re-layouts: 0.08 us -> 3.92 us  [the longest x1 1.41 us: fused_body(): queries.reshape(tok, heads * slots * width)]
  transfers between devices with their start and end apart: 3 -> 0, of which waited for: 3 -> 0; matrix products, arithmetic and copies ran while one was open for 3% -> 0% of each run, Pallas kernels for 0% -> 0%
where the time goes in v1:
time: 95.2 us; the launch traced here: 93.4 us
  Pallas kernels  87.1 us (91%)
  local copies, waits for them, and re-layouts  6.27 us (7%)
    pallas_call x1, Pallas kernels, fused_body(): pl.pallas_call(fused_kernel, out_shape=jax.ShapeDtypeStruct((tok, 2 * col...  87.1 us
    unnamed x11, local copies, waits for them, and re-layouts  2.34 us

profile of v1, /device:TPU:0, one launch (start us, length us, event | category | flops | bytes accessed | tf_op | source)
XLA Modules:
  0.0 93.4 jit_solution(18192858224307965187)
XLA Ops:
  0.0 0.0 copy-start
  0.0 0.0 copy-start.3
  0.0 0.0 copy-start.2
  0.0 0.0 copy-start.1
  0.0 1.1 %reshape.11.c_ref = bf16[2,2,32,512]{3,2,1,0:T(8,128)(2,1)S(1)} reshape(bf16[2,2,32,4,128]{4,3,2,1,0:T(4,128)(2,1)} %param.11) | data formatting | bytes 262144 | tf_op jit(solution)/shard_map/reshape | solution.py:418
  1.1 0.8 copy.10.ex_ref
  1.9 0.8 copy.11.ga_ref
  2.8 1.4 %reshape.9.q_ref = bf16[256,1024]{1,0:T(8,128)(2,1)S(1)} reshape(bf16[256,4,2,128]{3,2,1,0:T(2,128)(2,1)} %param.9) | data formatting | bytes 1048576 | tf_op jit(solution)/shard_map/reshape | solution.py:416
  4.2 1.4 %reshape.10.s_ref = bf16[256,1024]{1,0:T(8,128)(2,1)S(1)} reshape(bf16[256,2,4,128]{3,2,1,0:T(4,128)(2,1)} %param.10) | data formatting | bytes 1048576 | tf_op jit(solution)/shard_map/reshape | solution.py:417
  5.6 0.0 copy-done
  5.6 0.0 copy-done.3
  5.6 0.0 copy-done.2
  5.6 0.0 copy-done.1
  5.6 87.1 %shard_map.91 = bf16[256,512]{1,0:T(8,128)(2,1)S(1)} custom-call(s32[16]{0:T(128)S(1)} %copy-done.1, s32[4]{0:T(128)S(1)} %copy-done.2, s32[1,4]{1,0:T(1,128)S(1)} %copy-done.3, s32[256,2]{1,0:T(8,128)S(1)} %copy.10.ex_ref, f32[256,2]{1,0:T(8,128)S(1)} %copy.11.ga_ref, bf16[256,1024]{1,0:T(8,128)(2,1)S(1)} %reshape.9.q_ref, ...), custom_call_target="tpu_custom_call" | custom-call | flops 6000000000 | bytes 8000000 | tf_op jit(solution)/shard_map/pallas_call | solution.py:391
  92.7 0.7 copy.13
Async XLA Ops:
  0.0 5.6 %copy-start = (bf16[8,256,512]{2,1,0:T(8,128)(2,1)S(1)}, bf16[8,256,512]{2,1,0:T(8,128)(2,1)}, u32[]{:S(2)}) copy-start(bf16[8,256,512]{2,1,0:T(8,128)(2,1)} %w_ref.1) | copy-start | bytes 6291460
  0.0 5.6 %copy-start.3 = (s32[1,4]{1,0:T(1,128)S(1)}, s32[1,4]{1,0:T(1,128)}, u32[]{:S(2)}) copy-start(s32[1,4]{1,0:T(1,128)} %sl_ref.1) | copy-start | bytes 52
  0.0 5.6 %copy-start.2 = (s32[4]{0:T(128)S(1)}, s32[4]{0:T(128)}, u32[]{:S(2)}) copy-start(s32[4]{0:T(128)} %rp_ref.1) | copy-start | bytes 52
  0.0 5.6 %copy-start.1 = (s32[16]{0:T(128)S(1)}, s32[16]{0:T(128)}, u32[]{:S(2)}) copy-start(s32[16]{0:T(128)} %pt_ref.1) | copy-start | bytes 196

commit v2 on v1

--- a/solution.py
+++ b/solution.py
@@ -127,6 +127,7 @@
     return lax.psum_scatter(column_sums.astype(jnp.bfloat16), "kv", scatter_dimension=1, tiled=True)
 
 
+EARLY = 1
 MESH = pl.DeviceIdType.MESH
 F32 = jnp.float32
 BF16 = jnp.bfloat16
@@ -185,11 +186,16 @@
     own_w = pltpu.make_async_copy(w_ref, wbuf.at[0], loc_sem.at[1])
     own_w.start()
 
-    lane = lax.broadcasted_iota(jnp.int32, (tok, 128), 1)
-    hot0 = jnp.where(lane == ex_ref[:, 0:1], 1.0, 0.0)
-    hot1 = jnp.where(lane - 8 == ex_ref[:, 1:2], 1.0, 0.0)
-    hot = jnp.where(lane < 8, hot0, jnp.where(lane < 16, hot1, 0.0))
-    tbl[z] = hot.T[0:16].astype(BF16)
+    def wcopy(e):
+        return remote(w_ref.at[e], wbuf.at[1, e], w_send.at[e], w_recv.at[e], (partner, k))
+
+    for e in range(EARLY):
+        wcopy(e).start()
+
+    expert = lax.broadcasted_iota(jnp.int32, (8, tok), 0)
+    for j in range(2):
+        tbl[z, j * 8 : (j + 1) * 8] = jnp.where(expert == ex_ref[j : j + 1, :], 1.0, 0.0).astype(BF16)
+    gates = [jnp.broadcast_to(ga_ref[j : j + 1, :], (128, tok)).T for j in range(2)]
 
     def tcopy(d, slot):
         return remote(tbl.at[slot], tbl.at[slot], t_send.at[d - 1], t_recv.at[d - 1], (zpeer(d) * 2 + y, k))
@@ -215,29 +221,34 @@
     keep = jnp.logical_and(req_row[:, 0:1] == req_col[0:1, :], row[:, 0:1] >= colq[0:1, :])
     bias[:, cached:] = jnp.where(keep, 0.0, MASKED_SCORE)
 
+    own_c.wait()
     for d in (1, 3, 2):
-        cz(d, lax.rem(z - d + 4, 4) * 2 + y).wait_recv()
+        slot = lax.rem(z - d + 4, 4) * 2 + y
+        cz(d, slot).wait_recv()
         cy(d).start()
-    own_c.wait()
-
-    def wcopy():
-        return remote(w_ref, wbuf.at[1], w_send.at[0], w_recv.at[0], (partner, k))
-
-    wcopy().start()
+    for e in range(EARLY, 8):
+        wcopy(e).start()
     for d in (1, 2, 3):
         tcopy(d, z).start()
-
-    def ycopy_in(d):
+    for d in (0, 1, 3, 2):
         slot = lax.rem(z - d + 4, 4) * 2 + (1 - y)
-        return remote(cbuf.at[slot], cbuf.at[slot], cy_send.at[d], cy_recv.at[d], (partner, k))
-
-    for d in range(4):
-        ycopy_in(d).wait_recv()
-
-    def ucopy(h, d, slot):
+        remote(cbuf.at[slot], cbuf.at[slot], cy_send.at[d], cy_recv.at[d], (partner, k)).wait_recv()
+
+    def ulink(way, source, h):
+        to = z + 1 - 2 * way
         return remote(
-            ubuf.at[slot, h], ubuf.at[slot, h], u_send.at[h, d - 1], u_recv.at[h, d - 1], (zpeer(d) * 2 + y, k)
-        )
+            ubuf.at[source, h], ubuf.at[source, h], u_send.at[way, source, h], u_recv.at[source, h], (to * 2 + y, k)
+        )
+
+    inner = jnp.logical_and(z > 0, z < 3)
+
+    def pass_on(h):
+        @pl.when(inner)
+        def _():
+            ulink(0, z - 1, h).wait_recv()
+            ulink(0, z - 1, h).start()
+            ulink(1, z + 1, h).wait_recv()
+            ulink(1, z + 1, h).start()
 
     factor = math.log2(math.e) / math.sqrt(128)
     for h in range(heads):
@@ -247,8 +258,7 @@
         skeys = s_ref[:, span]
         svalues = s_ref[:, heads * 128 + h * 128 : heads * 128 + (h + 1) * 128]
         for j in range(2):
-            place = slice((h * 2 + j) * 128, (h * 2 + j + 1) * 128)
-            query = q_ref[:, place]
+            query = q_ref[:, (h * 2 + j) * 128 : (h * 2 + j + 1) * 128]
             sa = lax.dot_general(query, keys, NT, preferred_element_type=F32) * factor + bias[:, 0:cached]
             sb = lax.dot_general(query, skeys, NT, preferred_element_type=F32) * factor + bias[:, cached:]
             top = jnp.maximum(jnp.max(sa, axis=1, keepdims=True), jnp.max(sb, axis=1, keepdims=True))
@@ -259,14 +269,29 @@
                 pb.astype(BF16), svalues, preferred_element_type=F32
             )
             att = (num / den).astype(BF16).astype(F32)
-            ubuf[z, h, :, j * 128 : (j + 1) * 128] = (att * ga_ref[:, j : j + 1]).astype(BF16)
-        for d in (1, 3, 2):
-            ucopy(h, d, z).start()
+            ubuf[z, h, :, j * 128 : (j + 1) * 128] = (att * gates[j]).astype(BF16)
+
+        @pl.when(z < 3)
+        def _():
+            ulink(0, z, h).start()
+
+        @pl.when(z > 0)
+        def _():
+            ulink(1, z, h).start()
+
+        if h > 0:
+            pass_on(h - 1)
     own_w.wait()
 
     sel_row = lax.broadcasted_iota(jnp.int32, (16, 16 * 128), 0)
     sel_col = lax.broadcasted_iota(jnp.int32, (16, 16 * 128), 1) // 128
     select = jnp.where(sel_row == sel_col, 1.0, 0.0).astype(BF16)
+
+    def source_of(i):
+        near = jnp.where(z < 2, z, 3 - z)
+        later = jnp.where(near == 0, i, i - 1 + i // 2)
+        base = jnp.where(i == 0, near, jnp.where(i == 3, 3, later))
+        return jnp.where(z < 2, base, 3 - base)
 
     def pcopy(i, e):
         q = lax.rem(k + e, 4)
@@ -275,31 +300,43 @@
             pbuf.at[i, rows], prec.at[i, e - 1], p_send.at[i, e - 1], p_recv.at[i, e - 1], (blk, q)
         )
 
-    def half_of(i):
-        half = jnp.where(i < 4, y, 1 - y)
+    def block_at(i):
+        return jnp.where(i < 6, lax.rem(i, 3), 3)
+
+    def side_at(i):
+        return jnp.where(i < 6, i // 3, i - 6)
+
+    def half_of(side):
+        half = jnp.where(side == 0, y, 1 - y)
         return pl.ds(pl.multiple_of(half * 256, 256), 256)
 
     def ocopy(i):
-        d = lax.rem(i, 4)
+        d = block_at(i)
         rows = pl.ds(pl.multiple_of(k * 64, 64), 64)
-        to = lax.rem(z - d + 4, 4) * 2 + y
-        return remote(fin.at[i], o_ref.at[rows, half_of(i)], o_send.at[i], o_recv.at[i // 4, k], (to, z))
+        to = source_of(d) * 2 + y
+        return remote(fin.at[i], o_ref.at[rows, half_of(side_at(i))], o_send.at[i], o_recv.at[side_at(i), k], (to, z))
 
     def step(i, carry):
         @pl.when(i < 8)
         def _():
-            d = lax.rem(i, 4)
-            source = lax.rem(z - d + 4, 4)
-
-            @pl.when(i < 4)
-            def _():
-                @pl.when(d > 0)
+            d = block_at(i)
+            side = side_at(i)
+            source = source_of(d)
+
+            @pl.when(side == 0)
+            def _():
+                @pl.when(d == 1)
+                def _():
+                    pass_on(heads - 1)
+                    for t in (1, 2, 3):
+                        tcopy(t, z).wait_recv()
+
+                @pl.when(jnp.logical_and(d > 0, jnp.logical_not(inner)))
                 def _():
                     for h in range(heads):
                         remote(
-                            ubuf.at[source, h], ubuf.at[source, h], u_send.at[h, d - 1], u_recv.at[h, d - 1], (blk, k)
+                            ubuf.at[source, h], ubuf.at[source, h], u_send.at[0, source, h], u_recv.at[source, h], (blk, k)
                         ).wait_recv()
-                    remote(tbl.at[source], tbl.at[source], t_send.at[d - 1], t_recv.at[d - 1], (blk, k)).wait_recv()
 
                 mask = lax.dot_general(
                     tbl[source], select, (((0,), (0,)), ((), ())), preferred_element_type=F32
@@ -312,14 +349,21 @@
                             u0 * mask[:, e * 128 : (e + 1) * 128] + u1 * mask[:, (8 + e) * 128 : (9 + e) * 128]
                         )
 
-            @pl.when(i == 4)
-            def _():
-                wcopy().wait_recv()
+            @pl.when(jnp.logical_and(i == 3, inner))
+            def _():
+                for h in range(heads):
+                    ulink(z % 2, source_of(3), h).wait_recv()
+                    ulink(z % 2, source_of(3), h).start()
+
+            @pl.when(i == 3)
+            def _():
+                for e in range(8):
+                    wcopy(e).wait_recv()
 
             part = jnp.zeros((tok, 256), F32)
             for e in range(8):
                 part = part + lax.dot_general(
-                    comb[d, :, e * 512 : (e + 1) * 512], wbuf[i // 4, e], NT, preferred_element_type=F32
+                    comb[d, :, e * 512 : (e + 1) * 512], wbuf[side, e], NT, preferred_element_type=F32
                 )
             pbuf[i] = part.astype(BF16)
             for e in (2, 3, 1):
@@ -333,11 +377,11 @@
             for e in (1, 2, 3):
                 pcopy(p, e).wait_recv()
                 total = total + prec[p, e - 1].astype(F32)
-            here = jnp.logical_and(lax.rem(p, 4) == 0, k == z)
+            here = jnp.logical_and(block_at(p) == 0, k == z)
 
             @pl.when(here)
             def _():
-                o_ref[own, half_of(p)] = total.astype(BF16)
+                o_ref[own, half_of(side_at(p))] = total.astype(BF16)
 
             @pl.when(jnp.logical_not(here))
             def _():
@@ -355,14 +399,14 @@
             @pl.when(jnp.logical_or(k != z, k != q))
             def _():
                 remote(
-                    fin.at[0], o_ref.at[rows, half_of(g * 4)], o_send.at[0], o_recv.at[g, q], (blk, k)
+                    fin.at[0], o_ref.at[rows, half_of(g)], o_send.at[0], o_recv.at[g, q], (blk, k)
                 ).wait_recv()
 
     def drain(i, carry):
         for e in (1, 2, 3):
             pcopy(i, e).wait_send()
 
-        @pl.when(jnp.logical_or(lax.rem(i, 4) != 0, k != z))
+        @pl.when(jnp.logical_or(block_at(i) != 0, k != z))
         def _():
             ocopy(i).wait_send()
 
@@ -372,11 +416,25 @@
     for d in (1, 2, 3):
         cz(d, blk).wait_send()
         tcopy(d, z).wait_send()
-        for h in range(heads):
-            ucopy(h, d, z).wait_send()
     for d in range(4):
         cy(d).wait_send()
-    wcopy().wait_send()
+    for e in range(8):
+        wcopy(e).wait_send()
+    for h in range(heads):
+
+        @pl.when(z < 3)
+        def _():
+            ulink(0, z, h).wait_send()
+
+        @pl.when(z > 0)
+        def _():
+            ulink(1, z, h).wait_send()
+
+        @pl.when(inner)
+        def _():
+            ulink(0, z - 1, h).wait_send()
+            ulink(1, z + 1, h).wait_send()
+            ulink(z % 2, source_of(3), h).wait_send()
 
 
 def fused_body(
@@ -403,8 +461,8 @@
             pltpu.VMEM((8, tok, columns), BF16),
             pltpu.VMEM((8, 3, tok // 4, columns), BF16),
             pltpu.VMEM((8, tok // 4, columns), BF16),
-            dma((2,)), dma((3,)), dma((3,)), dma((4,)), dma((4,)), dma((1,)), dma((1,)),
-            dma((3,)), dma((3,)), dma((heads, 3)), dma((heads, 3)),
+            dma((2,)), dma((3,)), dma((3,)), dma((4,)), dma((4,)), dma((experts,)), dma((experts,)),
+            dma((3,)), dma((3,)), dma((2, 4, heads)), dma((4, heads)),
             dma((8, 3)), dma((8, 3)), dma((8,)), dma((2, 4)),
         ],
         compiler_params=pltpu.CompilerParams(
@@ -412,7 +470,7 @@
         ),
         cost_estimate=pl.CostEstimate(flops=6 * 10**9, bytes_accessed=8 * 10**6, transcendentals=2 * 10**6),
     )(
-        page_table, req_prefix, suffix_len, att_experts, att_gates,
+        page_table, req_prefix, suffix_len, att_experts.T, att_gates.T,
         queries.reshape(tok, heads * slots * width),
         suffix_kv.reshape(tok, 2 * heads * width),
         cache.reshape(local_pages, 2, page_rows, heads * width),

time: 95.2 us -> 87.7 us (0.921)
  the two profiles are of different devices: /device:TPU:0 before, /device:TPU:24 now
where the time goes in v2:
time: 87.7 us; the launch traced here: 87.5 us
  Pallas kernels  82.8 us (94%)
  local copies, waits for them, and re-layouts  4.64 us (5%)
    pallas_call x1, Pallas kernels, fused_body(): pl.pallas_call(fused_kernel, out_shape=jax.ShapeDtypeStruct((tok, 2 * col...  82.8 us

profile of v2, /device:TPU:24, one launch (start us, length us, event | category | flops | bytes accessed | tf_op | source)
XLA Modules:
  0.0 87.5 jit_solution(5049624761013756682)
XLA Ops:
  0.0 0.0 copy-start
  0.0 0.0 copy-start.2
  0.0 0.0 copy-start.1
  0.0 0.0 copy-start.5
  0.0 0.0 copy-start.4
  0.0 0.0 copy-start.3
  0.0 1.1 %reshape.11.c_ref = bf16[2,2,32,512]{3,2,1,0:T(8,128)(2,1)S(1)} reshape(bf16[2,2,32,4,128]{4,3,2,1,0:T(4,128)(2,1)} %param.11) | data formatting | bytes 262144 | tf_op jit(solution)/shard_map/reshape | solution.py:476
  1.1 1.4 %reshape.9.q_ref = bf16[256,1024]{1,0:T(8,128)(2,1)S(1)} reshape(bf16[256,4,2,128]{3,2,1,0:T(2,128)(2,1)} %param.9) | data formatting | bytes 1048576 | tf_op jit(solution)/shard_map/reshape | solution.py:474
  2.6 1.4 %reshape.10.s_ref = bf16[256,1024]{1,0:T(8,128)(2,1)S(1)} reshape(bf16[256,2,4,128]{3,2,1,0:T(4,128)(2,1)} %param.10) | data formatting | bytes 1048576 | tf_op jit(solution)/shard_map/reshape | solution.py:475
  4.0 0.0 copy-done
  4.0 0.0 copy-done.2
  4.0 0.0 copy-done.1
  4.0 0.0 copy-done.5
  4.0 0.0 copy-done.4
  4.0 0.0 copy-done.3
  4.0 82.8 %shard_map.91 = bf16[256,512]{1,0:T(8,128)(2,1)S(1)} custom-call(s32[16]{0:T(128)S(1)} %copy-done.3, s32[4]{0:T(128)S(1)} %copy-done.4, s32[1,4]{1,0:T(1,128)S(1)} %copy-done.5, s32[2,256]{1,0:T(2,128)S(1)} %bitcast.2, f32[2,256]{1,0:T(2,128)S(1)} %bitcast.3, bf16[256,1024]{1,0:T(8,128)(2,1)S(1)} %reshape.9.q_ref, bf16[256,1024]{1,0:T(8,128)(2,1)S(1)} %reshape.10.s_ref, ...), custom_call_target="tpu_custom_call" | custom-call | flops 6000000000 | bytes 8000000 | tf_op jit(solution)/shard_map/pallas_call | solution.py:449
  86.8 0.7 copy.11
Async XLA Ops:
  0.0 4.0 %copy-start = (bf16[8,256,512]{2,1,0:T(8,128)(2,1)S(1)}, bf16[8,256,512]{2,1,0:T(8,128)(2,1)}, u32[]{:S(2)}) copy-start(bf16[8,256,512]{2,1,0:T(8,128)(2,1)} %w_ref.1) | copy-start | bytes 6291460
  0.0 4.0 %copy-start.2 = (f32[256,2]{0,1:T(2,128)S(1)}, f32[256,2]{0,1:T(2,128)}, u32[]{:S(2)}) copy-start(f32[256,2]{0,1:T(2,128)} %param.16) | copy-start | bytes 6148
  0.0 4.0 %copy-start.1 = (s32[256,2]{0,1:T(2,128)S(1)}, s32[256,2]{0,1:T(2,128)}, u32[]{:S(2)}) copy-start(s32[256,2]{0,1:T(2,128)} %param.15) | copy-start | bytes 6148
  0.0 4.0 %copy-start.5 = (s32[1,4]{1,0:T(1,128)S(1)}, s32[1,4]{1,0:T(1,128)}, u32[]{:S(2)}) copy-start(s32[1,4]{1,0:T(1,128)} %sl_ref.1) | copy-start | bytes 52
  0.0 4.0 %copy-start.4 = (s32[4]{0:T(128)S(1)}, s32[4]{0:T(128)}, u32[]{:S(2)}) copy-start(s32[4]{0:T(128)} %rp_ref.1) | copy-start | bytes 52
  0.0 4.0 %copy-start.3 = (s32[16]{0:T(128)S(1)}, s32[16]{0:T(128)}, u32[]{:S(2)}) copy-start(s32[16]{0:T(128)} %pt_ref.1) | copy-start | bytes 196
